TPU v7x, 32 devices: a whole 2x2x4 slice. The times are simulated.
32 devices in a mesh: rep: 2 (over y), ep: 8 (over z, x), tp: 2 (over core).
Axes of the slice: x: 2, y: 2, z: 4, core: 2. Of those that a mesh axis runs over, the one named last changes fastest.
Arguments:
- tokens: bfloat16 [2048, 6144], P(('rep', 'ep'), 'tp'), parts along dimension 0, may hold values from -6 to 6
- expert_ids: int32 [2048, 4], P(('rep', 'ep')), parts along dimension 0, may hold values from 0 to 15, as said below
- gate_int: int32 [2048, 4], P(('rep', 'ep')), parts along dimension 0, may hold values from 1 to 64
- w_gate: bfloat16 [8, 6144, 2688], P('ep', 'tp'), may hold values from -0.078125 to 0.078125
- w_up: bfloat16 [8, 6144, 2688], P('ep', 'tp'), may hold values from -0.078125 to 0.078125
- w_down: bfloat16 [8, 2688, 6144], P('ep', None, 'tp'), may hold values from -0.078125 to 0.078125
Outputs:
- combined: bfloat16 [2048, 6144], P(('rep', 'ep'), 'tp'), parts along dimension 0
There are 2 independent parts, one for each index of `rep`. A program takes and returns all parts, laid end to end along the dimension named above; an argument that names none is the same for every part. Nothing has to cross between parts.
Inputs may be any that keep to these rules, and one draw needn't show every extreme that they name: `expert_ids`: each row names 4 different experts. In the 128 rows of one index of ep, one held expert (the same in every block of a draw, drawn from the seed) is named by exactly 32 rows, and every other held expert by 1 to 16 rows.
All inputs are finite; a program needn't handle non-finite values.
Results may differ from a plain program's by a relative error of at most 0.0058.
Values may be sent and summed in bfloat16 or wider, within the bound.
A program may use at most 128 MiB of HBM per device.

v0:
```python
import jax
import jax.numpy as jnp
from jax import lax
from jax.sharding import PartitionSpec as P

HELD = 4
CAP = 32


def silu_product(gate_up):
    return (jax.nn.silu(gate_up[:, 0]) * gate_up[:, 1]).astype(jnp.bfloat16)


def expert_rows(received, w_gate, w_up, w_down):
    columns = received.shape[-1]
    leading = received.shape[:-1]
    flattened = received.reshape(-1, columns)
    gate_part = jnp.dot(flattened, w_gate[0], preferred_element_type=jnp.float32)
    up_part = jnp.dot(flattened, w_up[0], preferred_element_type=jnp.float32)
    gate_up = jnp.stack([gate_part, up_part], axis=1)
    summed_half = lax.psum_scatter(gate_up, "tp", scatter_dimension=2, tiled=True)
    hidden = lax.all_gather(silu_product(summed_half), "tp", axis=1, tiled=True)
    partial_value = jnp.dot(hidden, w_down[0], preferred_element_type=jnp.float32).astype(
        jnp.bfloat16
    )
    return partial_value.reshape(leading + (partial_value.shape[-1],))


def send_back(partial_value):
    return lax.all_to_all(partial_value, "ep", split_axis=0, concat_axis=0, tiled=True)


def shards(tokens, expert_ids, gate_int, w_gate, w_up, w_down):
    row_count = tokens.shape[0]
    experts = lax.broadcasted_iota(jnp.int32, (HELD, 1, 1), 0)
    named = expert_ids[None, :, :] == experts
    weighting = jnp.sum(
        jnp.where(named, gate_int[None, :, :].astype(jnp.float32) / 64.0, jnp.float32(0.0)), axis=2
    )
    chosen = jnp.any(named, axis=2).astype(jnp.int32)
    slot_of = jnp.cumsum(chosen, axis=1) - 1
    slot_ids = lax.broadcasted_iota(jnp.int32, (HELD, CAP, row_count), 1)
    placed = (chosen[:, None, :] == 1) & (slot_of[:, None, :] == slot_ids)
    outgoing = jnp.einsum(
        "ecr,rd->ecd", placed.astype(jnp.bfloat16), tokens, preferred_element_type=jnp.float32
    ).astype(jnp.bfloat16)
    members = lax.axis_size("ep") // HELD
    outgoing = jnp.repeat(outgoing, members, axis=0)
    received = lax.all_to_all(outgoing, "ep", split_axis=0, concat_axis=0, tiled=True)
    returned = send_back(expert_rows(received, w_gate, w_up, w_down))
    columns = returned.shape[-1]
    summed = jnp.sum(returned.reshape(HELD, members, CAP, columns).astype(jnp.float32), axis=1)
    weighted = placed.astype(jnp.float32) * weighting[:, None, :]
    combined = jnp.einsum("ecr,ecd->rd", weighted, summed, precision=lax.Precision.HIGHEST)
    return combined.astype(jnp.bfloat16)


def solution(mesh):
    return jax.shard_map(
        shards,
        mesh=mesh,
        in_specs=(
            P(("rep", "ep"), "tp"),
            P(("rep", "ep"), None),
            P(("rep", "ep"), None),
            P("ep", "tp", None),
            P("ep", "tp", None),
            P("ep", None, "tp"),
        ),
        out_specs=P(("rep", "ep"), "tp"),
        check_vma=False,
    )
```

profile of v0, /device:TPU:0, one launch (start us, length us, event | category | flops | bytes accessed | tf_op | source)
XLA Modules:
  0.0 190.8 jit_solution(18234494010422279342)
XLA Ops:
  6.5 0.0 copy-start
  6.5 0.0 all-reduce.3.cloned.1.call-start
  6.5 0.8 fusion.28
  7.3 0.3 reduce_window_sum.11
  7.6 0.0 copy-done
  7.7 0.4 convolution_convert_fusion
  8.0 0.2 broadcast_in_dim.22
  8.3 0.0 slice-start
  8.3 44.3 %all_to_all.10 = bf16[8,32,3072]{2,1,0:T(8,128)(2,1)S(1)} all-to-all(bf16[8,32,3072]{2,1,0:T(8,128)(2,1)S(1)} %bitcast.46), channel_id=1, replica_groups=mesh['rep'=2,'ep'=8,'tp'=2] {'ep'}, dimensions={0} | all-to-all | bytes 3145728 | tf_op jit(solution)/shard_map/all_to_all | solution.py:49
  52.6 0.0 slice-start.1
  52.6 0.0 slice-start.2
  52.6 0.0 slice-start.3
  52.6 8.9 %fusion.6 = f32[256,1,2688]{2,0,1:T(8,128)S(1)} fusion(bf16[256,3072]{1,0:T(8,128)(2,1)S(1)} %bitcast.47, bf16[1,3072,2688]{2,1,0:T(8,128)(2,1)} %param.9), kind=kOutput, calls=%fused_computation.7 | convolution fusion | flops 4227858432 | bytes 20840448 | tf_op jit(solution)/shard_map/dot_general | solution.py:18
  61.5 0.0 slice-done
  61.5 0.0 slice-done.1
  61.5 0.0 slice-done.2
  61.6 0.3 slice-done.3
  61.9 4.6 %fusion.9 = f32[256,1,2688]{2,0,1:T(8,128)S(1)} fusion(bf16[256,3072]{1,0:T(8,128)(2,1)S(1)} %bitcast.48, bf16[1,3072,2688]{2,1,0:T(8,128)(2,1)S(1)} %bitcast.50), kind=kOutput, calls=%fused_computation.8 | convolution fusion | flops 4227858432 | bytes 20840448 | tf_op jit(solution)/shard_map/dot_general | solution.py:19
  66.5 2.8 %pad_maximum_fusion = f32[256,2,2688]{2,0,1:T(8,128)} fusion(f32[256,1,2688]{2,0,1:T(8,128)S(1)} %fusion.9, f32[256,1,2688]{2,0,1:T(8,128)S(1)} %fusion.6), kind=kLoop, calls=%fused_computation.6 | loop fusion | flops 1376256 | bytes 11010048 | tf_op jit(solution)/shard_map/stack | solution.py:20
  69.4 9.4 %copy.13 = f32[256,2,2688]{0,1,2:T(2,128)} copy(f32[256,2,2688]{2,0,1:T(8,128)} %pad_maximum_fusion) | data formatting | bytes 11010048 | tf_op jit(solution)/shard_map/stack | solution.py:20
  78.8 0.0 copy-start.4
  78.8 0.0 all-reduce.3.cloned.1.call-update
  78.8 0.2 all-gather.2.cloned.1.call-start
  79.1 0.4 copy-done.4
  79.5 0.6 dynamic-slice
  80.7 27.9 %all-reduce.3.cloned.1.call-done = f32[256,2,2688]{0,1,2:T(2,128)} async-done(((f32[256,2,2688]{0,1,2:T(2,128)}), f32[256,2,2688]{0,1,2:T(2,128)}) %all-reduce.3.cloned.1.call-update) | async-done | bytes 5505040
  108.6 5.2 %constant_dynamic-slice_fusion = (f32[256,1,1344]{0,1,2:T(1,128)S(1)}, f32[256,1,1344]{0,1,2:T(1,128)S(1)}) fusion(f32[256,2,2688]{0,1,2:T(2,128)} %all-reduce.3.cloned.1.call-done, u32[]{:T(128)S(6)} %multiply.3, u32[]{:T(128)S(6)} %convert.2), kind=kLoop, calls=%fused_computation.33 | loop fusion | bytes 5505032 | tf_op jit(solution)/shard_map/slice | solution.py:11
  113.8 1.3 fusion.16
  115.1 0.0 all-gather.2.cloned.1.call-update
  115.1 10.9 %all-gather.2.cloned.1.call-done = bf16[256,2688]{0,1:T(8,128)(2,1)} async-done(((bf16[256,1344]{0,1:T(8,128)(2,1)}), bf16[256,2688]{0,1:T(8,128)(2,1)}) %all-gather.2.cloned.1.call-update) | async-done | bytes 1376272 | tf_op jit(solution)/shard_map/all_gather | solution.py:22
  125.9 12.0 %fusion.12 = bf16[256,3072]{1,0:T(8,128)(2,1)} fusion(bf16[256,2688]{0,1:T(8,128)(2,1)} %all-gather.2.cloned.1.call-done, bf16[1,2688,3072]{2,1,0:T(8,128)(2,1)} %param.11), kind=kOutput, calls=%fused_computation.9 | convolution fusion | flops 4228644864 | bytes 19464192 | tf_op jit(solution)/shard_map/dot_general | solution.py:23
  137.9 0.0 copy-start.3
  137.9 0.0 copy-start.2
  137.9 5.9 %all-to-all-start.1 = ((bf16[8,32,3072]{2,1,0:T(8,128)(2,1)}), bf16[8,32,3072]{2,1,0:T(8,128)(2,1)S(1)}, u32[]{:S(2)}, u32[]{:S(2)}) async-start(bf16[8,32,3072]{2,1,0:T(8,128)(2,1)} %bitcast.45), calls=%async_computation.1 | async-start | bytes 3145728 | tf_op jit(solution)/shard_map/all_to_all | solution.py:30
  143.8 0.0 copy-done.3
  143.9 0.0 copy-done.2
  143.9 37.4 %all-to-all-done.1 = bf16[8,32,3072]{2,1,0:T(8,128)(2,1)S(1)} async-done(((bf16[8,32,3072]{2,1,0:T(8,128)(2,1)}), bf16[8,32,3072]{2,1,0:T(8,128)(2,1)S(1)}, u32[]{:S(2)}, u32[]{:S(2)}) %all-to-all-start.1) | async-done | bytes 1572896 | tf_op jit(solution)/shard_map/all_to_all | solution.py:30
  181.3 0.0 copy-start.1
  181.3 0.3 convert_reduce_fusion
  181.6 2.4 %fusion.15 = bf16[128,3072]{1,0:T(8,128)(2,1)} fusion(f32[4,32,3072]{2,1,0:T(8,128)S(1)} %convert_reduce_fusion, f32[4,128]{1,0:T(4,128)S(1)} %select_reduce_fusion, s32[4,128]{1,0:T(4,128)S(1)} %broadcast_add_fusion, pred[4,128]{1,0:T(4,128)(4,1)S(1)} %get-tuple-element.7), kind=kOutput, calls=%fused_computation.11 | convolution fusion | flops 604422144 | bytes 2363904 | tf_op jit(solution)/shard_map/ecr,ecd->rd/dot_general | solution.py:54
  183.9 0.0 copy-done.1
  (5 shorter events, 0.0 us)
Async XLA Ops:
  6.5 1.1 copy-start
  6.5 102.1 %all-reduce.3.cloned.1.call-start = ((), (), s32[]{:S(2)}) async-start(), calls=%async_computation.3 | async-start | bytes 11010048
  8.3 53.3 %slice-start = ((s8[16515072]{0:T(1024)(128)(4,1)}), s8[4194304]{0:T(1024)(128)(4,1)S(1)}, s32[]{:S(2)}) async-start(s8[16515072]{0:T(1024)(128)(4,1)} %bitcast.49), calls=%async_computation.4 | async-start | bytes 8388608
  52.6 8.9 %slice-start.1 = ((s8[16515072]{0:T(1024)(128)(4,1)}), s8[4194304]{0:T(1024)(128)(4,1)S(1)}, s32[]{:S(2)}) async-start(s8[16515072]{0:T(1024)(128)(4,1)} %bitcast.49), calls=%async_computation.5 | async-start | bytes 8388608
  52.6 9.0 %slice-start.2 = ((s8[16515072]{0:T(1024)(128)(4,1)}), s8[4194304]{0:T(1024)(128)(4,1)S(1)}, s32[]{:S(2)}) async-start(s8[16515072]{0:T(1024)(128)(4,1)} %bitcast.49), calls=%async_computation.6 | async-start | bytes 8388608
  52.6 9.3 %slice-start.3 = ((s8[16515072]{0:T(1024)(128)(4,1)}), s8[3932160]{0:T(1024)(128)(4,1)S(1)}, s32[]{:S(2)}) async-start(s8[16515072]{0:T(1024)(128)(4,1)} %bitcast.49), calls=%async_computation.7 | async-start | bytes 7864320
  78.8 0.7 copy-start.4
  78.8 47.1 %all-gather.2.cloned.1.call-start = ((), (), s32[]{:S(2)}) async-start(), calls=%async_computation.2 | async-start | bytes 2064384 | tf_op jit(solution)/shard_map/all_gather | solution.py:22
  137.9 5.9 %copy-start.3 = (s32[128,4]{0,1:T(4,128)S(1)}, s32[128,4]{0,1:T(4,128)}, u32[]{:S(2)}) copy-start(s32[128,4]{0,1:T(4,128)} %param.8) | copy-start | bytes 6148
  137.9 5.9 %copy-start.2 = (s32[128,4]{0,1:T(4,128)S(1)}, s32[128,4]{0,1:T(4,128)}, u32[]{:S(2)}) copy-start(s32[128,4]{0,1:T(4,128)} %param.7) | copy-start | bytes 6148
  137.9 43.4 %all-to-all-start.1 = ((bf16[8,32,3072]{2,1,0:T(8,128)(2,1)}), bf16[8,32,3072]{2,1,0:T(8,128)(2,1)S(1)}, u32[]{:S(2)}, u32[]{:S(2)}) async-start(bf16[8,32,3072]{2,1,0:T(8,128)(2,1)} %bitcast.45), calls=%async_computation.1 | async-start | bytes 3145728 | tf_op jit(solution)/shard_map/all_to_all | solution.py:30
  181.3 2.6 %copy-start.1 = (bf16[128,3072]{1,0:T(8,128)(2,1)S(1)}, bf16[128,3072]{1,0:T(8,128)(2,1)}, u32[]{:S(2)}) copy-start(bf16[128,3072]{1,0:T(8,128)(2,1)} %param.6) | copy-start | bytes 2359300
Sparse Core Ops, SparseCore 0:
  78.9 29.6 all-reduce.2
  115.2 10.7 all-gather.1
where the time goes:
time: 191 us
  waiting for transfers between devices  76.2 us (40%)
  blocking collectives  44.3 us (23%)
  matrix products  28.3 us (15%)
  local copies, waits for them, and re-layouts  16.2 us (8%)
  between operations  14.2 us (7%)
  starting transfers between devices  6.12 us (3%)
  other arithmetic  5.48 us (3%)
    all_to_all x1, blocking collectives, shards(): lax.all_to_all(outgoing, 'ep', split_axis=0, concat_axis=0, tiled=True)  44.3 us
    all_to_all x1, waiting for transfers between devices, send_back(): lax.all_to_all(partial_value, 'ep', split_axis=0, concat_axis=0, tiled=True)  37.4 us
    unnamed x3, waiting for transfers between devices  27.9 us
    dot_general x1, matrix products, expert_rows(): jnp.dot(hidden, w_down[0], preferred_element_type=jnp.float32)  12 us
    all_gather x1, waiting for transfers between devices, expert_rows(): hidden = lax.all_gather(silu_product(summed_half), 'tp', axis=1, tiled=True)  10.9 us
    another operation x1, local copies, waits for them, and re-layouts, expert_rows(): gate_up = jnp.stack([gate_part, up_part], axis=1)  9.43 us
    dot_general x1, matrix products, expert_rows(): jnp.dot(flattened, w_gate[0], preferred_element_type=jnp.float32)  8.92 us
    all_to_all x1, starting transfers between devices, send_back(): lax.all_to_all(partial_value, 'ep', split_axis=0, concat_axis=0, tiled=True)  5.9 us
  transfers between devices with their start and end apart: 3, of which 3 were waited for; matrix products, arithmetic and copies ran while one was open for 0% of the time, Pallas kernels for 0%

commit v1 on v0

--- a/solution.py
+++ b/solution.py
@@ -1,10 +1,303 @@
+import functools
+
 import jax
 import jax.numpy as jnp
 from jax import lax
+from jax.experimental import pallas as pl
+from jax.experimental.pallas import tpu as pltpu
 from jax.sharding import PartitionSpec as P
 
 HELD = 4
 CAP = 32
+MEMBERS = 2
+K_CHUNKS = 4
+OUT_COLS = 512
+HID_COLS = 512
+DOWN_SLOTS = 3
+
+
+def remote(src, dst, send_sem, recv_sem, axis, index):
+    return pltpu.make_async_remote_copy(
+        src_ref=src,
+        dst_ref=dst,
+        send_sem=send_sem,
+        recv_sem=recv_sem,
+        device_id={axis: index},
+        device_id_type=pl.DeviceIdType.MESH,
+    )
+
+
+def fused_kernel(
+    ids_ref, gint_ref, tok_hbm, wg_hbm, wu_hbm, wd_hbm, out_ref,
+    tok, wg, wu, wd, send, recv, acc_g, acc_u, gu_send, gu_recv, hid,
+    part, part_in, own, total, ret,
+    tok_sem, wg_sem, wu_sem, wd_sem,
+    z_send, z_recv, x_send, x_recv, gu_ss, gu_rs, hid_ss, hid_rs,
+    px_send, px_recv, rz_send, rz_recv,
+):
+    rows, depth = tok.shape
+    hidden = wg.shape[1]
+    out_cols = wd.shape[2]
+    out_chunks = part.shape[0]
+    kw = depth // K_CHUNKS
+    half = HELD * CAP
+    me = lax.axis_index("ep")
+    mine = lax.div(me, MEMBERS)
+    x = lax.rem(me, MEMBERS)
+    t = lax.axis_index("tp")
+    x_peer = mine * MEMBERS + 1 - x
+    t_peer = 1 - t
+    my_row = pl.multiple_of(t * half, half)
+    peer_row = pl.multiple_of(t_peer * half, half)
+    full_tiles = hidden // HID_COLS
+    tail = hidden % HID_COLS
+
+    def z_to(d):
+        return lax.rem(mine + d, HELD)
+
+    def z_from(d):
+        return lax.rem(mine + HELD - d, HELD)
+
+    def over_tiles(body):
+        def step(n, carry):
+            body(n, pl.ds(pl.multiple_of(n * HID_COLS, HID_COLS), HID_COLS))
+            return carry
+
+        lax.fori_loop(0, full_tiles, step, 0)
+        if tail:
+            body(full_tiles, pl.ds(full_tiles * HID_COLS, tail))
+
+    tok_copy = pltpu.make_async_copy(tok_hbm, tok, tok_sem)
+    tok_copy.start()
+
+    def weight_copies(k):
+        band = pl.ds(k * kw, kw)
+        return (
+            pltpu.make_async_copy(wg_hbm.at[0, band], wg.at[band], wg_sem.at[k]),
+            pltpu.make_async_copy(wu_hbm.at[0, band], wu.at[band], wu_sem.at[k]),
+        )
+
+    def down_copy(c):
+        return pltpu.make_async_copy(
+            wd_hbm.at[0, :, pl.ds(c * out_cols, out_cols)],
+            wd.at[c % DOWN_SLOTS],
+            wd_sem.at[c % DOWN_SLOTS],
+        )
+
+    for k in range(K_CHUNKS):
+        for copy in weight_copies(k):
+            copy.start()
+    for c in range(min(DOWN_SLOTS, out_chunks)):
+        down_copy(c).start()
+
+    barrier = pltpu.get_barrier_semaphore()
+    for d in range(1, HELD):
+        pl.semaphore_signal(
+            barrier, inc=1, device_id={"ep": z_to(d) * MEMBERS + x},
+            device_id_type=pl.DeviceIdType.MESH,
+        )
+    pl.semaphore_signal(
+        barrier, inc=1, device_id={"ep": x_peer}, device_id_type=pl.DeviceIdType.MESH
+    )
+    pl.semaphore_signal(
+        barrier, inc=1, device_id={"tp": t_peer}, device_id_type=pl.DeviceIdType.MESH
+    )
+
+    lane = lax.broadcasted_iota(jnp.int32, (rows, half), 1)
+    lane_expert = lax.div(lane, CAP)
+    lane_slot = lax.rem(lane, CAP).astype(jnp.float32)
+    chosen = jnp.zeros((rows, half), jnp.float32)
+    weight = jnp.zeros((rows, half), jnp.float32)
+    for j in range(ids_ref.shape[1]):
+        hit = ids_ref[:, j : j + 1] == lane_expert
+        chosen = chosen + jnp.where(hit, 1.0, 0.0)
+        weight = weight + jnp.where(hit, gint_ref[:, j : j + 1].astype(jnp.float32) / 64.0, 0.0)
+    lower = (
+        lax.broadcasted_iota(jnp.int32, (rows, rows), 0)
+        >= lax.broadcasted_iota(jnp.int32, (rows, rows), 1)
+    )
+    rank = jnp.dot(
+        jnp.where(lower, 1.0, 0.0).astype(jnp.bfloat16),
+        chosen.astype(jnp.bfloat16),
+        preferred_element_type=jnp.float32,
+    )
+    placed = jnp.where(rank == lane_slot + 1.0, chosen, 0.0)
+    weighted = (placed * weight).astype(jnp.bfloat16)
+    placed = placed.astype(jnp.bfloat16)
+
+    pl.semaphore_wait(barrier, HELD + 1)
+    tok_copy.wait()
+
+    def z_copy(k, d):
+        return remote(
+            send.at[k, z_to(d)], recv.at[k, 0, mine], z_send.at[k, d - 1],
+            z_recv.at[k, d - 1], "ep", z_to(d) * MEMBERS + x,
+        )
+
+    def x_copy(k, d):
+        block = z_from(d)
+        return remote(
+            recv.at[k, 0, block], recv.at[k, 1, block], x_send.at[k, d],
+            x_recv.at[k, d], "ep", x_peer,
+        )
+
+    for k in range(K_CHUNKS):
+        packed = lax.dot_general(
+            placed, tok[:, k * kw : (k + 1) * kw], (((0,), (0,)), ((), ())),
+            preferred_element_type=jnp.float32,
+        ).astype(jnp.bfloat16)
+        send[k] = packed.reshape(HELD, CAP, kw)
+        for d in (2, 1, 3):
+            z_copy(k, d).start()
+        recv[k, 0, mine] = send[k, mine]
+        x_copy(k, 0).start()
+
+    def forward(k):
+        for d in (1, 3, 2):
+            z_copy(k, d).wait_recv()
+            x_copy(k, d).start()
+
+    def project(k):
+        for copy in weight_copies(k):
+            copy.wait()
+        for d in range(HELD):
+            x_copy(k, d).wait_recv()
+        band = pl.ds(k * kw, kw)
+
+        def tile(n, cols):
+            lhs = recv[k].reshape(MEMBERS * half, kw)
+            for w, acc in ((wg, acc_g), (wu, acc_u)):
+                value = jnp.dot(lhs, w[band, cols], preferred_element_type=jnp.float32)
+                if k > 0:
+                    value = value + acc[:, cols]
+                acc[:, cols] = value
+            if k == K_CHUNKS - 1:
+                for i, acc in enumerate((acc_g, acc_u)):
+                    gu_send[i, :, cols] = acc[pl.ds(peer_row, half), cols].astype(jnp.bfloat16)
+                gu_copy(n, cols).start()
+
+        over_tiles(tile)
+
+    def gu_copy(n, cols):
+        return remote(
+            gu_send.at[:, :, cols], gu_recv.at[:, :, cols], gu_ss.at[n], gu_rs.at[n], "tp", t_peer
+        )
+
+    def hid_copy(n, cols):
+        span = hid.at[pl.ds(my_row, half), cols]
+        return remote(span, span, hid_ss.at[n], hid_rs.at[n], "tp", t_peer)
+
+    forward(0)
+    for k in range(1, K_CHUNKS):
+        forward(k)
+        project(k - 1)
+    project(K_CHUNKS - 1)
+
+    def activate(n, cols):
+        gu_copy(n, cols).wait_recv()
+        gate = acc_g[pl.ds(my_row, half), cols] + gu_recv[0, :, cols].astype(jnp.float32)
+        up = acc_u[pl.ds(my_row, half), cols] + gu_recv[1, :, cols].astype(jnp.float32)
+        hid[pl.ds(my_row, half), cols] = (jax.nn.silu(gate) * up).astype(jnp.bfloat16)
+        hid_copy(n, cols).start()
+
+    over_tiles(activate)
+    over_tiles(lambda n, cols: hid_copy(n, cols).wait_recv())
+
+    def part_copy(c):
+        return remote(part.at[c], part_in.at[c], px_send.at[c], px_recv.at[c], "ep", x_peer)
+
+    def ret_copy(c, d):
+        return remote(
+            total.at[c, z_to(d)], ret.at[c, mine], rz_send.at[c, d - 1], rz_recv.at[c, d - 1],
+            "ep", z_to(d) * MEMBERS + x,
+        )
+
+    for c in range(out_chunks):
+        down_copy(c).wait()
+        value = jnp.dot(
+            hid[...], wd[c % DOWN_SLOTS], preferred_element_type=jnp.float32
+        ).astype(jnp.bfloat16)
+        part[c] = value[half:]
+        part_copy(c).start()
+        own[c] = value[:half]
+        if c + DOWN_SLOTS < out_chunks:
+            down_copy(c + DOWN_SLOTS).start()
+
+    for c in range(out_chunks):
+        part_copy(c).wait_recv()
+        value = (own[c].astype(jnp.float32) + part_in[c].astype(jnp.float32)).astype(jnp.bfloat16)
+        total[c] = value.reshape(HELD, CAP, out_cols)
+        for d in (2, 1, 3):
+            ret_copy(c, d).start()
+        ret[c, mine] = total[c, mine]
+
+    for c in range(out_chunks):
+        for d in range(1, HELD):
+            ret_copy(c, d).wait_recv()
+        out_ref[:, c * out_cols : (c + 1) * out_cols] = jnp.dot(
+            weighted, ret[c].reshape(half, out_cols), preferred_element_type=jnp.float32
+        ).astype(jnp.bfloat16)
+
+    for k in range(K_CHUNKS):
+        for d in range(HELD):
+            x_copy(k, d).wait_send()
+            if d > 0:
+                z_copy(k, d).wait_send()
+    over_tiles(lambda n, cols: gu_copy(n, cols).wait_send())
+    over_tiles(lambda n, cols: hid_copy(n, cols).wait_send())
+    for c in range(out_chunks):
+        part_copy(c).wait_send()
+        for d in range(1, HELD):
+            ret_copy(c, d).wait_send()
+
+
+def fused_shards(tokens, expert_ids, gate_int, w_gate, w_up, w_down):
+    rows, depth = tokens.shape
+    hidden = w_gate.shape[2]
+    columns = w_down.shape[2]
+    out_chunks = columns // OUT_COLS
+    half = HELD * CAP
+    kw = depth // K_CHUNKS
+    tiles = pl.cdiv(hidden, HID_COLS)
+    bf16, f32 = jnp.bfloat16, jnp.float32
+    dma = pltpu.SemaphoreType.DMA
+    return pl.pallas_call(
+        fused_kernel,
+        out_shape=jax.ShapeDtypeStruct((rows, columns), bf16),
+        in_specs=[pl.BlockSpec(memory_space=pltpu.VMEM)] * 2
+        + [pl.BlockSpec(memory_space=pl.ANY)] * 4,
+        out_specs=pl.BlockSpec(memory_space=pltpu.VMEM),
+        scratch_shapes=[
+            pltpu.VMEM((rows, depth), bf16),
+            pltpu.VMEM((depth, hidden), bf16),
+            pltpu.VMEM((depth, hidden), bf16),
+            pltpu.VMEM((DOWN_SLOTS, hidden, OUT_COLS), bf16),
+            pltpu.VMEM((K_CHUNKS, HELD, CAP, kw), bf16),
+            pltpu.VMEM((K_CHUNKS, MEMBERS, HELD, CAP, kw), bf16),
+            pltpu.VMEM((MEMBERS * half, hidden), f32),
+            pltpu.VMEM((MEMBERS * half, hidden), f32),
+            pltpu.VMEM((2, half, hidden), bf16),
+            pltpu.VMEM((2, half, hidden), bf16),
+            pltpu.VMEM((MEMBERS * half, hidden), bf16),
+            pltpu.VMEM((out_chunks, half, OUT_COLS), bf16),
+            pltpu.VMEM((out_chunks, half, OUT_COLS), bf16),
+            pltpu.VMEM((out_chunks, half, OUT_COLS), bf16),
+            pltpu.VMEM((out_chunks, HELD, CAP, OUT_COLS), bf16),
+            pltpu.VMEM((out_chunks, HELD, CAP, OUT_COLS), bf16),
+            dma, dma((K_CHUNKS,)), dma((K_CHUNKS,)), dma((DOWN_SLOTS,)),
+            dma((K_CHUNKS, HELD - 1)), dma((K_CHUNKS, HELD - 1)),
+            dma((K_CHUNKS, HELD)), dma((K_CHUNKS, HELD)),
+            dma((tiles,)), dma((tiles,)), dma((tiles,)), dma((tiles,)),
+            dma((out_chunks,)), dma((out_chunks,)),
+            dma((out_chunks, HELD - 1)), dma((out_chunks, HELD - 1)),
+        ],
+        compiler_params=pltpu.CompilerParams(
+            collective_id=0, has_side_effects=True, vmem_limit_bytes=64000000
+        ),
+        cost_estimate=pl.CostEstimate(
+            flops=12 * half * depth * hidden, bytes_accessed=6 * depth * hidden, transcendentals=0
+        ),
+    )(expert_ids, gate_int, tokens, w_gate, w_up, w_down)
 
 
 def silu_product(gate_up):
@@ -30,7 +323,21 @@
     return lax.all_to_all(partial_value, "ep", split_axis=0, concat_axis=0, tiled=True)
 
 
+def fits(tokens, w_gate, w_down):
+    depth, hidden = w_gate.shape[1:]
+    return (
+        lax.axis_size("ep") == HELD * MEMBERS
+        and lax.axis_size("tp") == 2
+        and tokens.shape[0] == HELD * CAP
+        and depth % (128 * K_CHUNKS) == 0
+        and hidden % 128 == 0
+        and w_down.shape[2] % OUT_COLS == 0
+    )
+
+
 def shards(tokens, expert_ids, gate_int, w_gate, w_up, w_down):
+    if fits(tokens, w_gate, w_down):
+        return fused_shards(tokens, expert_ids, gate_int, w_gate, w_up, w_down)
     row_count = tokens.shape[0]
     experts = lax.broadcasted_iota(jnp.int32, (HELD, 1, 1), 0)
     named = expert_ids[None, :, :] == experts

time: 191 us -> 76.6 us (0.40)
  waiting for transfers between devices: 76.2 us -> 0 us
  Pallas kernels: 0 us -> 71.4 us
  blocking collectives: 44.3 us -> 0 us
  matrix products: 28.3 us -> 0 us
  between operations: 14.2 us -> 0.01 us
  local copies, waits for them, and re-layouts: 16.2 us -> 4.88 us
  starting transfers between devices: 6.12 us -> 0 us
  other arithmetic: 5.48 us -> 0 us
    pallas_call x0 -> x1, Pallas kernels: none -> 71.4 us  [fused_shards(): pl.pallas_call(fused_kernel, out_shape=jax.ShapeDtypeStruct((rows, column...]
    all_to_all x1 -> x0, blocking collectives: 44.3 us -> none  [shards(): lax.all_to_all(outgoing, 'ep', split_axis=0, concat_axis=0, tiled=True)]
    all_to_all x1 -> x0, waiting for transfers between devices: 37.4 us -> none  [send_back(): lax.all_to_all(partial_value, 'ep', split_axis=0, concat_axis=0, tiled=True)]
    dot_general x5 -> x0, matrix products: 28.3 us -> none  [the longest x1 12 us: expert_rows(): jnp.dot(hidden, w_down[0], preferred_element_type=jnp.float32)]
    unnamed x3 -> x0, waiting for transfers between devices: 27.9 us -> none
    all_gather x1 -> x0, waiting for transfers between devices: 10.9 us -> none  [expert_rows(): hidden = lax.all_gather(silu_product(summed_half), 'tp', axis=1, tiled=True)]
    another operation x1 -> x0, local copies, waits for them, and re-layouts: 9.43 us -> none  [expert_rows(): gate_up = jnp.stack([gate_part, up_part], axis=1)]
    all_to_all x1 -> x0, starting transfers between devices: 5.9 us -> none  [send_back(): lax.all_to_all(partial_value, 'ep', split_axis=0, concat_axis=0, tiled=True)]
  transfers between devices with their start and end apart: 3 -> 0, of which waited for: 3 -> 0; matrix products, arithmetic and copies ran while one was open for 0% -> 0% of each run, Pallas kernels for 0% -> 0%
where the time goes in v1:
time: 76.6 us; the launch traced here: 76.3 us
  Pallas kernels  71.4 us (93%)
  local copies, waits for them, and re-layouts  4.88 us (6%)
    pallas_call x1, Pallas kernels, fused_shards(): pl.pallas_call(fused_kernel, out_shape=jax.ShapeDtypeStruct((rows, column...  71.4 us
    unnamed x3, local copies, waits for them, and re-layouts  4.88 us

profile of v1, /device:TPU:0, one launch (start us, length us, event | category | flops | bytes accessed | tf_op | source)
XLA Modules:
  0.0 76.3 jit_solution(3803367411653658461)
XLA Ops:
  0.0 1.4 %copy.7.ids_ref = s32[128,4]{1,0:T(8,128)} copy(s32[128,4]{0,1:T(4,128)} %param.7) | data formatting | bytes 4096 | tf_op args[1]
  1.4 1.4 %copy.8.gint_ref = s32[128,4]{1,0:T(8,128)} copy(s32[128,4]{0,1:T(4,128)} %param.8) | data formatting | bytes 4096 | tf_op args[2]
  2.8 71.4 %shard_map.64 = bf16[128,3072]{1,0:T(8,128)(2,1)} custom-call(s32[128,4]{1,0:T(8,128)} %copy.7.ids_ref, s32[128,4]{1,0:T(8,128)} %copy.8.gint_ref, bf16[128,3072]{1,0:T(8,128)(2,1)} %tok_hbm.1, bf16[1,3072,2688]{2,1,0:T(8,128)(2,1)} %wg_hbm.1, bf16[1,3072,2688]{2,1,0:T(8,128)(2,1)} %wu_hbm.1, bf16[1,2688,3072]{2,1,0:T(8,128)(2,1)} %wd_hbm.1), custom_call_target="tpu_custom_call" | custom-call | flops 12683575296 | bytes 49545216 | tf_op jit(solution)/shard_map/pallas_call | solution.py:264
  74.2 2.1 %copy.10 = bf16[128,3072]{1,0:T(8,128)(2,1)} copy(bf16[128,3072]{1,0:T(8,128)(2,1)} %shard_map.64) | data formatting | bytes 1572864

commit v2 on v1

--- a/solution.py
+++ b/solution.py
@@ -10,10 +10,10 @@
 HELD = 4
 CAP = 32
 MEMBERS = 2
-K_CHUNKS = 4
-OUT_COLS = 512
+K_CHUNKS = 3
+OUT_COLS = 768
 HID_COLS = 512
-DOWN_SLOTS = 3
+DOWN_SLOTS = 2
 
 
 def remote(src, dst, send_sem, recv_sem, axis, index):
@@ -103,26 +103,26 @@
         barrier, inc=1, device_id={"tp": t_peer}, device_id_type=pl.DeviceIdType.MESH
     )
 
-    lane = lax.broadcasted_iota(jnp.int32, (rows, half), 1)
-    lane_expert = lax.div(lane, CAP)
-    lane_slot = lax.rem(lane, CAP).astype(jnp.float32)
-    chosen = jnp.zeros((rows, half), jnp.float32)
-    weight = jnp.zeros((rows, half), jnp.float32)
-    for j in range(ids_ref.shape[1]):
-        hit = ids_ref[:, j : j + 1] == lane_expert
+    spot = lax.broadcasted_iota(jnp.int32, (half, rows), 0)
+    spot_expert = lax.div(spot, CAP)
+    spot_slot = lax.rem(spot, CAP).astype(jnp.float32)
+    chosen = jnp.zeros((half, rows), jnp.float32)
+    weight = jnp.zeros((half, rows), jnp.float32)
+    for j in range(ids_ref.shape[0]):
+        hit = ids_ref[j : j + 1] == spot_expert
         chosen = chosen + jnp.where(hit, 1.0, 0.0)
-        weight = weight + jnp.where(hit, gint_ref[:, j : j + 1].astype(jnp.float32) / 64.0, 0.0)
-    lower = (
+        weight = weight + jnp.where(hit, gint_ref[j : j + 1].astype(jnp.float32) / 64.0, 0.0)
+    upper = (
         lax.broadcasted_iota(jnp.int32, (rows, rows), 0)
-        >= lax.broadcasted_iota(jnp.int32, (rows, rows), 1)
+        <= lax.broadcasted_iota(jnp.int32, (rows, rows), 1)
     )
     rank = jnp.dot(
-        jnp.where(lower, 1.0, 0.0).astype(jnp.bfloat16),
         chosen.astype(jnp.bfloat16),
+        jnp.where(upper, 1.0, 0.0).astype(jnp.bfloat16),
         preferred_element_type=jnp.float32,
     )
-    placed = jnp.where(rank == lane_slot + 1.0, chosen, 0.0)
-    weighted = (placed * weight).astype(jnp.bfloat16)
+    placed = jnp.where(rank == spot_slot + 1.0, chosen, 0.0)
+    weighted = jnp.transpose(placed * weight).astype(jnp.bfloat16)
     placed = placed.astype(jnp.bfloat16)
 
     pl.semaphore_wait(barrier, HELD + 1)
@@ -142,9 +142,8 @@
         )
 
     for k in range(K_CHUNKS):
-        packed = lax.dot_general(
-            placed, tok[:, k * kw : (k + 1) * kw], (((0,), (0,)), ((), ())),
-            preferred_element_type=jnp.float32,
+        packed = jnp.dot(
+            placed, tok[:, k * kw : (k + 1) * kw], preferred_element_type=jnp.float32
         ).astype(jnp.bfloat16)
         send[k] = packed.reshape(HELD, CAP, kw)
         for d in (2, 1, 3):
@@ -297,7 +296,7 @@
         cost_estimate=pl.CostEstimate(
             flops=12 * half * depth * hidden, bytes_accessed=6 * depth * hidden, transcendentals=0
         ),
-    )(expert_ids, gate_int, tokens, w_gate, w_up, w_down)
+    )(expert_ids.T, gate_int.T, tokens, w_gate, w_up, w_down)
 
 
 def silu_product(gate_up):

time: 76.6 us -> 72.8 us (0.950)
  local copies, waits for them, and re-layouts: 4.88 us -> 2.06 us
  Pallas kernels: 71.4 us -> 70.5 us
    unnamed x3 -> x1, local copies, waits for them, and re-layouts: 4.88 us -> 2.06 us
    pallas_call x1, Pallas kernels: 71.4 us -> 70.5 us  [fused_shards(): pl.pallas_call(fused_kernel, out_shape=jax.ShapeDtypeStruct((rows, column...]
where the time goes in v2:
time: 72.8 us; the launch traced here: 72.6 us
  Pallas kernels  70.5 us (97%)
  local copies, waits for them, and re-layouts  2.06 us (3%)
    pallas_call x1, Pallas kernels, fused_shards(): pl.pallas_call(fused_kernel, out_shape=jax.ShapeDtypeStruct((rows, column...  70.5 us
    unnamed x1, local copies, waits for them, and re-layouts  2.06 us

profile of v2, /device:TPU:0, one launch (start us, length us, event | category | flops | bytes accessed | tf_op | source)
XLA Modules:
  0.0 72.6 jit_solution(17310424858546627947)
XLA Ops:
  0.0 70.5 %shard_map.64 = bf16[128,3072]{1,0:T(8,128)(2,1)} custom-call(s32[4,128]{1,0:T(4,128)} %bitcast.2, s32[4,128]{1,0:T(4,128)} %bitcast.3, bf16[128,3072]{1,0:T(8,128)(2,1)} %tok_hbm.1, bf16[1,3072,2688]{2,1,0:T(8,128)(2,1)} %wg_hbm.1, bf16[1,3072,2688]{2,1,0:T(8,128)(2,1)} %wu_hbm.1, bf16[1,2688,3072]{2,1,0:T(8,128)(2,1)} %wd_hbm.1), custom_call_target="tpu_custom_call" | custom-call | flops 12683575296 | bytes 49545216 | tf_op jit(solution)/shard_map/pallas_call | solution.py:263
  70.5 2.1 %copy.8 = bf16[128,3072]{1,0:T(8,128)(2,1)} copy(bf16[128,3072]{1,0:T(8,128)(2,1)} %shard_map.64) | data formatting | bytes 1572864

commit v3 on v2

--- a/solution.py
+++ b/solution.py
@@ -12,7 +12,7 @@
 MEMBERS = 2
 K_CHUNKS = 3
 OUT_COLS = 768
-HID_COLS = 512
+HID_COLS = 768
 DOWN_SLOTS = 2
 
 

time: 72.8 us -> 72.5 us (level)
  no operation moved by 1% of the time
where the time goes in v3:
time: 72.5 us; the launch traced here: 72.3 us
  Pallas kernels  70.2 us (97%)
  local copies, waits for them, and re-layouts  2.06 us (3%)
    pallas_call x1, Pallas kernels, fused_shards(): pl.pallas_call(fused_kernel, out_shape=jax.ShapeDtypeStruct((rows, column...  70.2 us
    unnamed x1, local copies, waits for them, and re-layouts  2.06 us

profile of v3, /device:TPU:0, one launch (start us, length us, event | category | flops | bytes accessed | tf_op | source)
XLA Modules:
  0.0 72.3 jit_solution(11884783202014291535)
XLA Ops:
  0.0 70.2 %shard_map.64 = bf16[128,3072]{1,0:T(8,128)(2,1)} custom-call(s32[4,128]{1,0:T(4,128)} %bitcast.2, s32[4,128]{1,0:T(4,128)} %bitcast.3, bf16[128,3072]{1,0:T(8,128)(2,1)} %tok_hbm.1, bf16[1,3072,2688]{2,1,0:T(8,128)(2,1)} %wg_hbm.1, bf16[1,3072,2688]{2,1,0:T(8,128)(2,1)} %wu_hbm.1, bf16[1,2688,3072]{2,1,0:T(8,128)(2,1)} %wd_hbm.1), custom_call_target="tpu_custom_call" | custom-call | flops 12683575296 | bytes 49545216 | tf_op jit(solution)/shard_map/pallas_call | solution.py:263
  70.2 2.1 %copy.8 = bf16[128,3072]{1,0:T(8,128)(2,1)} copy(bf16[128,3072]{1,0:T(8,128)(2,1)} %shard_map.64) | data formatting | bytes 1572864
